TPU v7x, 32 devices: a whole 2x2x4 slice. The times are simulated.
32 devices in a mesh: slide: 4 (over z), strip: 8 (over y, x, core).
Axes of the slice: x: 2, y: 2, z: 4, core: 2. Of those that a mesh axis runs over, the one named last changes fastest.
Arguments:
- image: bfloat16 [4, 48, 16, 256], P('slide', 'strip'), may hold values from -6 to 6
- cotangent: bfloat16 [4, 48, 16, 256], P('slide', 'strip'), may hold values from -6 to 6
- kernel_tall: bfloat16 [51, 5, 256], replicated, may hold values from -0.375 to 0.375
- kernel_wide: bfloat16 [5, 51, 256], replicated, may hold values from -0.375 to 0.375
- layer_norm_gain: float32 [256], replicated, may hold values from 0.5 to 1.5
- layer_norm_bias: float32 [256], replicated, may hold values from -3 to 3
- w_in: bfloat16 [256, 1024], replicated, may hold values from -0.375 to 0.375
- b_in: float32 [1024], replicated, may hold values from -3 to 3
- w_out: bfloat16 [1024, 256], replicated, may hold values from -0.1875 to 0.1875
- b_out: float32 [256], replicated, may hold values from -3 to 3
Outputs:
- output: bfloat16 [4, 48, 16, 256], P('slide', 'strip')
- grad_image: bfloat16 [4, 48, 16, 256], P('slide', 'strip')
- grad_tall: float32 [51, 5, 256], replicated
- grad_wide: float32 [5, 51, 256], replicated
- grad_gain: float32 [256], replicated
- grad_shift: float32 [256], replicated
- grad_w_in: float32 [256, 1024], replicated
- grad_b_in: float32 [1024], replicated
- grad_w_out: float32 [1024, 256], replicated
- grad_b_out: float32 [256], replicated
All inputs are finite; a program needn't handle non-finite values.
Results may differ from a plain program's by a relative error of at most 0.0085.
Values may be sent and summed in bfloat16 or wider, within the bound.
A program may use at most 64 MiB of HBM per device.

v0:
```python
import jax
import jax.numpy as jnp
from jax import lax
from jax.sharding import PartitionSpec as P

epsilon = 1e-06


def for_sending(x):
    return jax.tree.map(lambda a: a.astype(jnp.bfloat16) if a.dtype == jnp.float32 else a, x)


def padded_2(cells, sides, width):
    for axis, dim in sides:
        count = lax.axis_size(axis)
        ends = count - 1
        head = lax.slice_in_dim(cells, 0, width, axis=dim)
        tail = lax.slice_in_dim(cells, cells.shape[dim] - width, cells.shape[dim], axis=dim)
        cells = jnp.concatenate(
            [
                lax.ppermute(tail, axis, [(i, (i + 1) % count) for i in range(ends)]),
                cells,
                lax.ppermute(head, axis, [((i + 1) % count, i) for i in range(ends)]),
            ],
            axis=dim,
        )
    return cells


def depth_conv(source, kernel, pad_rows, pad_cols):
    return lax.conv_general_dilated(
        source[None],
        kernel[:, :, None, :],
        (1, 1),
        ((pad_rows, pad_rows), (pad_cols, pad_cols)),
        dimension_numbers=("NHWC", "HWIO", "NHWC"),
        feature_group_count=source.shape[-1],
        preferred_element_type=jnp.float32,
    )[0]


def kernel_grad(padded, upstream):
    return lax.conv_general_dilated(
        padded[None],
        upstream[:, :, None, :],
        (1, 1),
        "VALID",
        dimension_numbers=("NHWC", "HWIO", "NHWC"),
        feature_group_count=padded.shape[-1],
        preferred_element_type=jnp.float32,
    )[0]


def to_columns(source, rim_width):
    turned = jax.tree.map(
        lambda part, own: part.astype(own.dtype),
        lax.all_to_all(for_sending(source), "strip", split_axis=1, concat_axis=0, tiled=True),
        source,
    )
    return padded_2(for_sending(turned), (("strip", 1),), rim_width).astype(turned.dtype)


def to_rows(source):
    return jax.tree.map(
        lambda part, own: part.astype(own.dtype),
        lax.all_to_all(for_sending(source), "strip", split_axis=0, concat_axis=1, tiled=True),
        source,
    )


def row_rims(source, rim_width):
    return padded_2(for_sending(source), (("strip", 0),), rim_width).astype(source.dtype)


def rows_margin(source, rim_width):
    return row_rims(to_rows(source), rim_width)


def local(
    image,
    cotangent,
    kernel_tall,
    kernel_wide,
    layer_norm_gain,
    layer_norm_bias,
    w_in,
    b_in,
    w_out,
    b_out,
):
    source = image[0]
    upstream = cotangent[0]
    row_count, full_width, channels = source.shape
    tall_pad = (kernel_tall.shape[0] - 1) // 2
    rim_width = (kernel_tall.shape[1] - 1) // 2
    wide_pad = (kernel_wide.shape[1] - 1) // 2
    scale_multiplier = jnp.float32(
        row_count * full_width * lax.axis_size("slide") * lax.axis_size("strip")
    ) ** (-0.5)
    tall_cols = to_columns(source, rim_width)
    mixed_cols = depth_conv(tall_cols, kernel_tall, tall_pad, 0).astype(jnp.bfloat16)
    mixed_rows = rows_margin(mixed_cols, rim_width)
    conv_out = depth_conv(mixed_rows, kernel_wide, 0, wide_pad)
    mean_removed = conv_out - jnp.mean(conv_out, axis=-1, keepdims=True)
    inverse_deviation = lax.rsqrt(
        jnp.mean(mean_removed * mean_removed, axis=-1, keepdims=True) + epsilon
    )
    standardized_input = mean_removed * inverse_deviation
    normalized_output = (standardized_input * layer_norm_gain + layer_norm_bias).astype(
        jnp.bfloat16
    )
    flat_normed = normalized_output.reshape(-1, channels)
    pre_act = jnp.dot(flat_normed, w_in, preferred_element_type=jnp.float32) + b_in
    cdf_value = 0.5 * (1.0 + lax.erf(pre_act * 0.7071067811865476))
    hidden = (pre_act * cdf_value).astype(jnp.bfloat16)
    branch = jnp.dot(hidden, w_out, preferred_element_type=jnp.float32) + b_out
    output = (source.astype(jnp.float32) + branch.reshape(source.shape)).astype(jnp.bfloat16)
    flat_cot = upstream.reshape(-1, channels)
    g_w_out = jnp.dot(hidden.T, flat_cot, preferred_element_type=jnp.float32) * scale_multiplier
    g_b_out = jnp.sum(flat_cot.astype(jnp.float32), axis=0) * scale_multiplier
    d_hidden = jnp.dot(flat_cot, w_out.T, preferred_element_type=jnp.float32)
    slope = cdf_value + pre_act * jnp.exp(-0.5 * pre_act * pre_act) * 0.3989422804014327
    d_pre = (d_hidden * slope).astype(jnp.bfloat16)
    g_w_in = jnp.dot(flat_normed.T, d_pre, preferred_element_type=jnp.float32) * scale_multiplier
    g_b_in = jnp.sum(d_pre.astype(jnp.float32), axis=0) * scale_multiplier
    grad_layer_norm = jnp.dot(d_pre, w_in.T, preferred_element_type=jnp.float32).reshape(
        source.shape
    )
    grad_norm_gain = jnp.sum(grad_layer_norm * standardized_input, axis=(0, 1)) * scale_multiplier
    g_shift = jnp.sum(grad_layer_norm, axis=(0, 1)) * scale_multiplier
    grad_standardized = grad_layer_norm * layer_norm_gain
    grad_depth_output = (
        inverse_deviation
        * (
            grad_standardized
            - jnp.mean(grad_standardized, axis=-1, keepdims=True)
            - standardized_input
            * jnp.mean(grad_standardized * standardized_input, axis=-1, keepdims=True)
        )
    ).astype(jnp.bfloat16)
    d_conv_rims = row_rims(grad_depth_output, rim_width)
    d_mixed = depth_conv(d_conv_rims, kernel_wide[::-1, ::-1], 0, wide_pad).astype(jnp.bfloat16)
    g_wide = (
        kernel_grad(jnp.pad(mixed_rows, ((0, 0), (wide_pad, wide_pad), (0, 0))), grad_depth_output)
        * scale_multiplier
    )
    d_mixed_cols = to_columns(d_mixed, rim_width)
    g_tall = (
        kernel_grad(
            jnp.pad(tall_cols, ((tall_pad, tall_pad), (0, 0), (0, 0))),
            d_mixed_cols[:, rim_width:-rim_width],
        )
        * scale_multiplier
    )
    d_image_cols = depth_conv(d_mixed_cols, kernel_tall[::-1, ::-1], tall_pad, 0).astype(
        jnp.bfloat16
    )
    d_image = to_rows(d_image_cols)
    grad_image = (upstream.astype(jnp.float32) + d_image.astype(jnp.float32)).astype(jnp.bfloat16)
    g_tall, g_wide, grad_norm_gain, g_shift, g_w_in, g_b_in, g_w_out, g_b_out = lax.psum(
        (g_tall, g_wide, grad_norm_gain, g_shift, g_w_in, g_b_in, g_w_out, g_b_out),
        ("slide", "strip"),
    )
    return (
        output[None],
        grad_image[None],
        g_tall,
        g_wide,
        grad_norm_gain,
        g_shift,
        g_w_in,
        g_b_in,
        g_w_out,
        g_b_out,
    )


def solution(mesh):
    placed = (
        P("slide", "strip", None, None),
        P("slide", "strip", None, None),
        P(),
        P(),
        P(),
        P(),
        P(),
        P(),
        P(),
        P(),
    )
    return jax.shard_map(
        local,
        mesh=mesh,
        in_specs=placed,
        out_specs=(
            P("slide", "strip", None, None),
            P("slide", "strip", None, None),
            P(),
            P(),
            P(),
            P(),
            P(),
            P(),
            P(),
            P(),
        ),
        check_vma=False,
    )
```

profile of v0, /device:TPU:0, one launch (start us, length us, event | category | flops | bytes accessed | tf_op | source)
XLA Modules:
  0.0 242.7 jit_solution(2152126875589892645)
XLA Ops:
  8.1 10.0 %all_to_all.63 = bf16[6,16,256]{2,0,1:T(8,128)(2,1)S(1)} all-to-all(bf16[6,16,256]{2,0,1:T(8,128)(2,1)S(1)} %bitcast.102), channel_id=1, replica_groups=mesh['slide'=4,'strip'=8] {'strip'}, dimensions={1} | all-to-all | bytes 98304 | tf_op jit(solution)/shard_map/all_to_all | solution.py:57
  18.1 1.4 collective-permute-start.1
  19.5 3.0 %collective-permute-start = (bf16[48,2,256]{2,1,0:T(2,128)(2,1)S(1)}, bf16[48,2,256]{2,1,0:T(2,128)(2,1)S(1)}, u32[]{:S(2)}, u32[]{:S(2)}) collective-permute-start(bf16[48,2,256]{2,1,0:T(2,128)(2,1)S(1)} %bitcast.106), channel_id=1, source_target_pairs={{0,1},{1,2},{2,3},{3,4},{4,5},{5,6},{6,7},{8,9},{9,10},{10,11},{11... | collective-permute-start | bytes 147464 | tf_op jit(solution)/shard_map/ppermute | solution.py:21
  23.6 7.2 %convolution_convert_fusion.2 = bf16[1,48,2,256]{3,0,2,1:T(2,128)(2,1)S(1)} fusion(bf16[1,48,6,256]{3,2,1,0:T(8,128)(2,1)S(1)} %get-tuple-element.33, bf16[51,5,1,256]{3,0,1,2:T(8,128)(2,1)S(1)} %bitcast.115), kind=kOutput, calls=%fused_computation.8 | convolution fusion | flops 9230336 | bytes 327168 | tf_op jit(solution)/shard_map/conv_general_dilated | solution.py:31
  31.5 5.9 %all-to-all-start.1 = ((bf16[48,2,256]{2,1,0:T(2,128)(2,1)}), bf16[48,2,256]{2,1,0:T(2,128)(2,1)S(1)}, u32[]{:S(2)}, u32[]{:S(2)}) async-start(bf16[48,2,256]{2,1,0:T(2,128)(2,1)} %copy.105), calls=%async_computation.1 | async-start | bytes 98304 | tf_op jit(solution)/shard_map/all_to_all | solution.py:66
  38.5 3.8 %all-to-all-done.1 = bf16[48,2,256]{2,1,0:T(2,128)(2,1)S(1)} async-done(((bf16[48,2,256]{2,1,0:T(2,128)(2,1)}), bf16[48,2,256]{2,1,0:T(2,128)(2,1)S(1)}, u32[]{:S(2)}, u32[]{:S(2)}) %all-to-all-start.1) | async-done | bytes 49184 | tf_op jit(solution)/shard_map/all_to_all | solution.py:66
  42.3 1.6 collective-permute-start.2
  45.4 2.2 collective-permute-done.3
  47.7 3.5 %fusion.34 = (f32[6,16]{1,0:T(8,128)S(1)}, f32[1,6,16,256]{3,0,2,1:T(1,128)S(1)}) fusion(bf16[5,51,1,256]{3,1,0,2:T(8,128)(2,1)S(1)} %bitcast.116, bf16[1,10,16,256]{3,2,1,0:T(8,128)(2,1)S(1)} %bitcast.119), kind=kOutput, calls=%fused_computation.82 | convolution fusion | flops 3956640 | bytes 311168 | tf_op jit(solution)/shard_map/conv_general_dilated | solution.py:31
  56.3 4.4 %collective-permute-start.4 = (bf16[2,16,256]{2,1,0:T(8,128)(2,1)S(1)}, bf16[2,16,256]{2,1,0:T(8,128)(2,1)S(1)}, u32[]{:S(2)}, u32[]{:S(2)}) collective-permute-start(bf16[2,16,256]{2,1,0:T(8,128)(2,1)S(1)} %get-tuple-element.36), channel_id=1, source_target_pairs={{0,1},{1,2},{2,3},{3,4},{4,5},{5,6},{6,7},{8,9},{9,10},{10,11},{11... | collective-permute-start | bytes 49160 | tf_op jit(solution)/shard_map/ppermute | solution.py:21
  60.7 1.5 collective-permute-start.5
  63.5 3.7 %convolution_multiply_fusion.3 = f32[1,5,51,256]{3,0,2,1:T(1,128)S(1)} fusion(bf16[1,10,66,256]{3,2,1,0:T(8,128)(2,1)S(1)} %pad_bitcast_fusion.1, f32[1,6,16,256]{3,0,2,1:T(1,128)S(1)} %get-tuple-element.41, f32[6,16,1,256]{3,2,1,0:T(1,128)S(1)} %reshape.154, f32[6,16]{1,0:T(8,128)S(1)} %div.24, f32[6,16]{1,0:T(8,128)S(1)} %broadcast_multiply_fusion.1, ...), kind=kOutput, calls=%fused_computation.9 | convolution fusion | flops 12795648 | bytes 798208 | tf_op jit(solution)/shard_map/conv_general_dilated | solution.py:43
  67.5 2.5 %convolution_convert_fusion.1 = bf16[1,6,16,256]{3,0,2,1:T(2,128)(2,1)S(1)} fusion(bf16[5,51,1,256]{3,1,0,2:T(8,128)(2,1)S(1)} %bitcast.118, bf16[1,10,16,256]{3,2,1,0:T(8,128)(2,1)S(1)} %maximum_bitcast_fusion.1), kind=kOutput, calls=%fused_computation.7 | convolution fusion | flops 3956736 | bytes 261632 | tf_op jit(solution)/shard_map/conv_general_dilated | solution.py:31
  70.7 5.5 %all-to-all-start.2 = ((bf16[6,16,256]{2,0,1:T(8,128)(2,1)}), bf16[6,16,256]{2,0,1:T(8,128)(2,1)S(1)}, u32[]{:S(2)}, u32[]{:S(2)}) async-start(bf16[6,16,256]{2,0,1:T(8,128)(2,1)} %bitcast.90), calls=%async_computation.2 | async-start | bytes 131072 | tf_op jit(solution)/shard_map/all_to_all | solution.py:57
  77.6 3.6 %all-to-all-done.2 = bf16[6,16,256]{2,0,1:T(8,128)(2,1)S(1)} async-done(((bf16[6,16,256]{2,0,1:T(8,128)(2,1)}), bf16[6,16,256]{2,0,1:T(8,128)(2,1)S(1)}, u32[]{:S(2)}, u32[]{:S(2)}) %all-to-all-start.2) | async-done | bytes 49184 | tf_op jit(solution)/shard_map/all_to_all | solution.py:57
  82.5 3.3 %collective-permute-start.6 = (bf16[48,2,256]{2,1,0:T(2,128)(2,1)S(1)}, bf16[48,2,256]{2,1,0:T(2,128)(2,1)S(1)}, u32[]{:S(2)}, u32[]{:S(2)}) collective-permute-start(bf16[48,2,256]{2,1,0:T(2,128)(2,1)S(1)} %bitcast.112), channel_id=1, source_target_pairs={{0,1},{1,2},{2,3},{3,4},{4,5},{5,6},{6,7},{8,9},{9,10},{10,11},{11... | collective-permute-start | bytes 147464 | tf_op jit(solution)/shard_map/ppermute | solution.py:21
  85.8 4.7 %convolution_multiply_fusion.4 = f32[1,51,5,256]{3,0,2,1:T(1,128)S(1)} fusion(bf16[1,98,6,256]{3,2,1,0:T(8,128)(2,1)S(1)} %pad_bitcast_fusion, bf16[48,2,1,256]{3,1,0,2:T(2,128)(2,1)S(1)} %bitcast.113), kind=kOutput, calls=%fused_computation.10 | convolution fusion | flops 12599040 | bytes 611328 | tf_op jit(solution)/shard_map/conv_general_dilated | solution.py:43
  91.4 7.2 %convolution_convert_fusion = bf16[1,48,2,256]{3,0,2,1:T(2,128)(2,1)S(1)} fusion(bf16[1,48,6,256]{3,2,1,0:T(8,128)(2,1)S(1)} %maximum_bitcast_fusion, bf16[51,5,1,256]{3,0,1,2:T(8,128)(2,1)S(1)} %bitcast.117), kind=kOutput, calls=%fused_computation.6 | convolution fusion | flops 9230336 | bytes 327168 | tf_op jit(solution)/shard_map/conv_general_dilated | solution.py:31
  99.3 3.5 %all-to-all-start.3 = ((bf16[48,2,256]{2,1,0:T(2,128)(2,1)}), bf16[48,2,256]{2,1,0:T(2,128)(2,1)S(1)}, u32[]{:S(2)}, u32[]{:S(2)}) async-start(bf16[48,2,256]{2,1,0:T(2,128)(2,1)} %copy.121), calls=%async_computation.3 | async-start | bytes 98304 | tf_op jit(solution)/shard_map/all_to_all | solution.py:66
  102.8 5.1 %all-to-all-done.3 = bf16[48,2,256]{2,1,0:T(2,128)(2,1)S(1)} async-done(((bf16[48,2,256]{2,1,0:T(2,128)(2,1)}), bf16[48,2,256]{2,1,0:T(2,128)(2,1)S(1)}, u32[]{:S(2)}, u32[]{:S(2)}) %all-to-all-start.3) | async-done | bytes 49184 | tf_op jit(solution)/shard_map/all_to_all | solution.py:66
  108.7 39.6 %all-reduce.2 = (f32[256]{0:T(256)}, f32[256]{0:T(256)}, f32[1024]{0:T(1024)}, f32[256]{0:T(256)}) all-reduce(f32[256]{0:T(256)S(1)} %get-tuple-element.48, f32[256]{0:T(256)S(1)} %get-tuple-element.47, f32[1024]{0:T(1024)S(1)} %broadcast_multiply_fusion, ...), channel_id=1, replica_groups=mesh['slide'=4,'strip'=8] {'slide','strip'}, use_global_device_ids=true, to_apply=%region_7.0 | all-reduce | flops 1792 | bytes 14336 | tf_op jit(solution)/shard_map/psum | solution.py:160
  148.3 81.5 %all-reduce.6.cloned.1.call-done = (f32[51,5,256]{2,0,1:T(8,128)}, f32[5,51,256]{2,1,0:T(8,128)}, f32[256,1024]{1,0:T(8,128)}, f32[1024,256]{1,0:T(8,128)}) async-done(((f32[51,5,256]{2,0,1:T(8,128)}, f32[5,51,256]{2,1,0:T(8,128)}, f32[256,1024]{1,0:T(8,128)}, f32[1024,256]{1,0:T(8,128)}), (f32[51,5,256]{2,0,1:T(8,128)}, f32[5,51,256]{2,1,0:T(8,128)}, f32[256,1024]{1,0:T(8,128)}, ...) | async-done | bytes 2619408 | tf_op jit(solution)/shard_map/psum | solution.py:160
  229.8 1.8 copy.185
  231.6 1.7 copy.186
  (90 shorter events, 20.1 us)
Async XLA Ops:
  7.2 45.1 %copy-start = (bf16[256,1024]{1,0:T(8,128)(2,1)S(1)}, bf16[256,1024]{1,0:T(8,128)(2,1)}, u32[]{:S(2)}) copy-start(bf16[256,1024]{1,0:T(8,128)(2,1)} %param.16) | copy-start | bytes 1572868
  18.1 5.5 %copy-start.6 = (bf16[51,5,256]{2,0,1:T(8,128)(2,1)S(1)}, bf16[51,5,256]{2,0,1:T(8,128)(2,1)}, u32[]{:S(2)}) copy-start(bf16[51,5,256]{2,0,1:T(8,128)(2,1)} %param.12) | copy-start | bytes 391684
  18.1 4.5 %collective-permute-start.1 = (bf16[48,2,256]{2,1,0:T(2,128)(2,1)S(1)}, bf16[48,2,256]{2,1,0:T(2,128)(2,1)S(1)}, u32[]{:S(2)}, u32[]{:S(2)}) collective-permute-start(bf16[48,2,256]{2,1,0:T(2,128)(2,1)S(1)} %bitcast.105), channel_id=1, source_target_pairs={{1,0},{2,1},{3,2},{4,3},{5,4},{6,5},{7,6},{9,8},{10,9},{11,10},{12... | collective-permute-start | bytes 147464 | tf_op jit(solution)/shard_map/ppermute | solution.py:23
  19.5 3.9 %collective-permute-start = (bf16[48,2,256]{2,1,0:T(2,128)(2,1)S(1)}, bf16[48,2,256]{2,1,0:T(2,128)(2,1)S(1)}, u32[]{:S(2)}, u32[]{:S(2)}) collective-permute-start(bf16[48,2,256]{2,1,0:T(2,128)(2,1)S(1)} %bitcast.106), channel_id=1, source_target_pairs={{0,1},{1,2},{2,3},{3,4},{4,5},{5,6},{6,7},{8,9},{9,10},{10,11},{11... | collective-permute-start | bytes 147464 | tf_op jit(solution)/shard_map/ppermute | solution.py:21
  31.5 10.8 %all-to-all-start.1 = ((bf16[48,2,256]{2,1,0:T(2,128)(2,1)}), bf16[48,2,256]{2,1,0:T(2,128)(2,1)S(1)}, u32[]{:S(2)}, u32[]{:S(2)}) async-start(bf16[48,2,256]{2,1,0:T(2,128)(2,1)} %copy.105), calls=%async_computation.1 | async-start | bytes 98304 | tf_op jit(solution)/shard_map/all_to_all | solution.py:66
  37.4 0.9 copy-start.7
  42.3 3.1 %collective-permute-start.2 = (bf16[2,16,256]{2,0,1:T(2,128)(2,1)S(1)}, bf16[2,16,256]{2,0,1:T(2,128)(2,1)S(1)}, u32[]{:S(2)}, u32[]{:S(2)}) collective-permute-start(bf16[2,16,256]{2,0,1:T(2,128)(2,1)S(1)} %bitcast.121), channel_id=1, source_target_pairs={{0,1},{1,2},{2,3},{3,4},{4,5},{5,6},{6,7},{8,9},{9,10},{10,11},{11... | collective-permute-start | bytes 49160 | tf_op jit(solution)/shard_map/ppermute | solution.py:21
  44.1 3.6 %collective-permute-start.3 = (bf16[2,16,256]{2,1,0:T(8,128)(2,1)S(1)}, bf16[2,16,256]{2,1,0:T(8,128)(2,1)S(1)}, u32[]{:S(2)}, u32[]{:S(2)}) collective-permute-start(bf16[2,16,256]{2,1,0:T(8,128)(2,1)S(1)} %copy.109), channel_id=1, source_target_pairs={{1,0},{2,1},{3,2},{4,3},{5,4},{6,5},{7,6},{9,8},{10,9},{11,10},{12... | collective-permute-start | bytes 49160 | tf_op jit(solution)/shard_map/ppermute | solution.py:23
  51.5 0.7 copy-start.8
  51.5 0.7 copy-start.10
  52.2 0.7 copy-start.9
  52.9 1.0 copy-start.3
  52.9 1.0 copy-start.4
  56.3 11.1 %collective-permute-start.4 = (bf16[2,16,256]{2,1,0:T(8,128)(2,1)S(1)}, bf16[2,16,256]{2,1,0:T(8,128)(2,1)S(1)}, u32[]{:S(2)}, u32[]{:S(2)}) collective-permute-start(bf16[2,16,256]{2,1,0:T(8,128)(2,1)S(1)} %get-tuple-element.36), channel_id=1, source_target_pairs={{0,1},{1,2},{2,3},{3,4},{4,5},{5,6},{6,7},{8,9},{9,10},{10,11},{11... | collective-permute-start | bytes 49160 | tf_op jit(solution)/shard_map/ppermute | solution.py:21
  60.7 6.8 %collective-permute-start.5 = (bf16[2,16,256]{2,1,0:T(8,128)(2,1)S(1)}, bf16[2,16,256]{2,1,0:T(8,128)(2,1)S(1)}, u32[]{:S(2)}, u32[]{:S(2)}) collective-permute-start(bf16[2,16,256]{2,1,0:T(8,128)(2,1)S(1)} %get-tuple-element.37), channel_id=1, source_target_pairs={{1,0},{2,1},{3,2},{4,3},{5,4},{6,5},{7,6},{9,8},{10,9},{11,10},{12... | collective-permute-start | bytes 49160 | tf_op jit(solution)/shard_map/ppermute | solution.py:23
  63.5 3.7 %copy-start.11 = (f32[256]{0:T(256)S(1)}, f32[256]{0:T(256)}, u32[]{:S(2)}) copy-start(f32[256]{0:T(256)} %param.19) | copy-start | bytes 3076
  70.7 5.5 %copy-start.5 = (bf16[1,6,16,256]{3,2,1,0:T(8,128)(2,1)S(1)}, bf16[1,6,16,256]{3,2,1,0:T(8,128)(2,1)}, u32[]{:S(2)}) copy-start(bf16[1,6,16,256]{3,2,1,0:T(8,128)(2,1)} %param.10) | copy-start | bytes 147460
  70.7 10.5 %all-to-all-start.2 = ((bf16[6,16,256]{2,0,1:T(8,128)(2,1)}), bf16[6,16,256]{2,0,1:T(8,128)(2,1)S(1)}, u32[]{:S(2)}, u32[]{:S(2)}) async-start(bf16[6,16,256]{2,0,1:T(8,128)(2,1)} %bitcast.90), calls=%async_computation.2 | async-start | bytes 131072 | tf_op jit(solution)/shard_map/all_to_all | solution.py:57
  76.2 153.6 %all-reduce.6.cloned.1.call-start = ((), (), s32[]{:S(2)}) async-start(), calls=%async_computation.4 | async-start | bytes 5341184 | tf_op jit(solution)/shard_map/psum | solution.py:160
  81.2 10.0 %collective-permute-start.7 = (bf16[48,2,256]{2,1,0:T(2,128)(2,1)S(1)}, bf16[48,2,256]{2,1,0:T(2,128)(2,1)S(1)}, u32[]{:S(2)}, u32[]{:S(2)}) collective-permute-start(bf16[48,2,256]{2,1,0:T(2,128)(2,1)S(1)} %bitcast.111), channel_id=1, source_target_pairs={{1,0},{2,1},{3,2},{4,3},{5,4},{6,5},{7,6},{9,8},{10,9},{11,10},{12... | collective-permute-start | bytes 147464 | tf_op jit(solution)/shard_map/ppermute | solution.py:23
  82.5 8.7 %collective-permute-start.6 = (bf16[48,2,256]{2,1,0:T(2,128)(2,1)S(1)}, bf16[48,2,256]{2,1,0:T(2,128)(2,1)S(1)}, u32[]{:S(2)}, u32[]{:S(2)}) collective-permute-start(bf16[48,2,256]{2,1,0:T(2,128)(2,1)S(1)} %bitcast.112), channel_id=1, source_target_pairs={{0,1},{1,2},{2,3},{3,4},{4,5},{5,6},{6,7},{8,9},{9,10},{10,11},{11... | collective-permute-start | bytes 147464 | tf_op jit(solution)/shard_map/ppermute | solution.py:21
  99.3 8.6 %all-to-all-start.3 = ((bf16[48,2,256]{2,1,0:T(2,128)(2,1)}), bf16[48,2,256]{2,1,0:T(2,128)(2,1)S(1)}, u32[]{:S(2)}, u32[]{:S(2)}) async-start(bf16[48,2,256]{2,1,0:T(2,128)(2,1)} %copy.121), calls=%async_computation.3 | async-start | bytes 98304 | tf_op jit(solution)/shard_map/all_to_all | solution.py:66
  229.8 3.5 %copy-start.2 = (f32[256,1024]{1,0:T(8,128)S(1)}, f32[256,1024]{1,0:T(8,128)}, u32[]{:S(2)}) copy-start(f32[256,1024]{1,0:T(8,128)} %get-tuple-element.57) | copy-start | bytes 3145732
  233.3 1.6 copy-start.1
Sparse Core Ops, SparseCore 0:
  91.4 138.3 all-reduce.5
where the time goes:
time: 244 us; the launch traced here: 243 us
  waiting for transfers between devices  97.1 us (40%)
  blocking collectives  49.6 us (20%)
  starting transfers between devices  32.6 us (13%)
  matrix products  32.5 us (13%)
  between operations  14.5 us (6%)
  local copies, waits for them, and re-layouts  14.3 us (6%)
    psum x1, waiting for transfers between devices, local(): lax.psum((g_tall, g_wide, grad_norm_gain, g_shift, g_w_in, g_b_in, g_w_ou...  81.5 us
    psum x1, blocking collectives, local(): lax.psum((g_tall, g_wide, grad_norm_gain, g_shift, g_w_in, g_b_in, g_w_ou...  39.6 us
    conv_general_dilated x4, matrix products, depth_conv(): lax.conv_general_dilated(source[None], kernel[:, :, None, :], (1, 1), ((p...  20.3 us
    ppermute x4, starting transfers between devices, padded_2(): lax.ppermute(tail, axis, [(i, (i + 1) % count) for i in range(ends)])  12.3 us
    unnamed x33, local copies, waits for them, and re-layouts  10.3 us
    all_to_all x1, blocking collectives, to_columns(): lax.all_to_all(for_sending(source), 'strip', split_axis=1, concat_axis=0,...  9.99 us
    all_to_all x2, starting transfers between devices, to_rows(): lax.all_to_all(for_sending(source), 'strip', split_axis=0, concat_axis=1,...  9.39 us
    all_to_all x2, waiting for transfers between devices, to_rows(): lax.all_to_all(for_sending(source), 'strip', split_axis=0, concat_axis=1,...  8.92 us
  transfers between devices with their start and end apart: 12, of which 6 were waited for; matrix products, arithmetic and copies ran while one was open for 9% of the time, Pallas kernels for 0%

commit v1 on v0

--- a/solution.py
+++ b/solution.py
@@ -1,30 +1,328 @@
+import functools
+
 import jax
 import jax.numpy as jnp
 from jax import lax
+from jax.experimental import pallas as pl
+from jax.experimental.pallas import tpu as pltpu
 from jax.sharding import PartitionSpec as P
 
 epsilon = 1e-06
-
-
-def for_sending(x):
-    return jax.tree.map(lambda a: a.astype(jnp.bfloat16) if a.dtype == jnp.float32 else a, x)
-
-
-def padded_2(cells, sides, width):
-    for axis, dim in sides:
-        count = lax.axis_size(axis)
-        ends = count - 1
-        head = lax.slice_in_dim(cells, 0, width, axis=dim)
-        tail = lax.slice_in_dim(cells, cells.shape[dim] - width, cells.shape[dim], axis=dim)
-        cells = jnp.concatenate(
-            [
-                lax.ppermute(tail, axis, [(i, (i + 1) % count) for i in range(ends)]),
-                cells,
-                lax.ppermute(head, axis, [((i + 1) % count, i) for i in range(ends)]),
-            ],
-            axis=dim,
-        )
-    return cells
+vmem_bytes = 48 * 1024 * 1024
+MESH = pl.DeviceIdType.MESH
+
+
+def enter(peers):
+    barrier = pltpu.get_barrier_semaphore()
+    for peer in peers:
+        pl.semaphore_signal(barrier, inc=1, device_id=peer, device_id_type=MESH)
+    pl.semaphore_wait(barrier, len(peers))
+
+
+def send(src, dst, send_sem, recv_sem, index, peer):
+    copy = pltpu.make_async_remote_copy(
+        src_ref=src,
+        dst_ref=dst,
+        send_sem=send_sem.at[index],
+        recv_sem=recv_sem.at[index],
+        device_id=peer,
+        device_id_type=MESH,
+    )
+    copy.start()
+    return copy
+
+
+def gather_kernel(count, own_ref, all_ref, send_sem, recv_sem):
+    me = lax.axis_index("strip")
+    peers = [{"strip": lax.rem(me + step, count)} for step in range(1, count)]
+    enter(peers)
+    copies = [
+        send(own_ref, all_ref.at[me], send_sem, recv_sem, index, peer)
+        for index, peer in enumerate(peers)
+    ]
+    all_ref[me] = own_ref[...]
+    for copy in copies:
+        copy.wait()
+
+
+def gather_rows(own, collective_id):
+    count = lax.axis_size("strip")
+    rows, width, channels = own.shape
+    gathered = pl.pallas_call(
+        functools.partial(gather_kernel, count),
+        out_shape=jax.ShapeDtypeStruct((count, rows * width, channels), own.dtype),
+        in_specs=[pl.BlockSpec(memory_space=pltpu.VMEM)],
+        out_specs=pl.BlockSpec(memory_space=pltpu.VMEM),
+        scratch_shapes=[
+            pltpu.SemaphoreType.DMA((count - 1,)),
+            pltpu.SemaphoreType.DMA((count - 1,)),
+        ],
+        compiler_params=pltpu.CompilerParams(
+            collective_id=collective_id, has_side_effects=True, vmem_limit_bytes=vmem_bytes
+        ),
+    )(own.reshape(rows * width, channels))
+    return gathered.reshape(count * rows, width, channels)
+
+
+def rim_kernel(count, size, own_ref, rims_ref, send_sem, recv_sem):
+    me = lax.axis_index("strip")
+    after = {"strip": lax.rem(me + 1, count)}
+    before = {"strip": lax.rem(me + count - 1, count)}
+    total = own_ref.shape[0]
+    enter([after, before])
+    copies = [
+        send(own_ref.at[pl.ds(total - size, size)], rims_ref.at[0], send_sem, recv_sem, 0, after),
+        send(own_ref.at[pl.ds(0, size)], rims_ref.at[1], send_sem, recv_sem, 1, before),
+    ]
+    for copy in copies:
+        copy.wait()
+
+
+def add_rims(own, rim_width, collective_id):
+    count = lax.axis_size("strip")
+    me = lax.axis_index("strip")
+    rows, width, channels = own.shape
+    size = rim_width * width
+    rims = pl.pallas_call(
+        functools.partial(rim_kernel, count, size),
+        out_shape=jax.ShapeDtypeStruct((2, size, channels), own.dtype),
+        in_specs=[pl.BlockSpec(memory_space=pltpu.VMEM)],
+        out_specs=pl.BlockSpec(memory_space=pltpu.VMEM),
+        scratch_shapes=[pltpu.SemaphoreType.DMA((2,)), pltpu.SemaphoreType.DMA((2,))],
+        compiler_params=pltpu.CompilerParams(
+            collective_id=collective_id, has_side_effects=True, vmem_limit_bytes=vmem_bytes
+        ),
+    )(own.reshape(rows * width, channels))
+    rims = rims.reshape(2, rim_width, width, channels)
+    above = jnp.where(me > 0, rims[0], 0)
+    below = jnp.where(me < count - 1, rims[1], 0)
+    return jnp.concatenate([above, own, below], axis=0)
+
+
+def sum_kernel(
+    strips,
+    slides,
+    groups,
+    w_in_ref,
+    w_out_ref,
+    rest_ref,
+    own_ref,
+    w_in_sum,
+    w_out_sum,
+    rest_sum,
+    all_ref,
+    total,
+    outbox,
+    inbox,
+    slide_out,
+    slide_in,
+    joint,
+    result,
+    send_sem,
+    recv_sem,
+    own_send_sem,
+    own_recv_sem,
+):
+    me = lax.axis_index("strip")
+    slide = lax.axis_index("slide")
+    channels = total.shape[1]
+    bits = [1 << k for k in range(strips.bit_length() - 1)]
+    orders = (bits, bits[:1] + bits[:0:-1])
+    mine = {bit: lax.rem(me // bit, 2) for bit in bits}
+    partner = {bit: {"strip": me + bit - 2 * bit * mine[bit]} for bit in bits}
+    neighbours = [{"strip": lax.rem(me + step, strips)} for step in range(1, strips)]
+    others = [{"slide": lax.rem(slide + step, slides)} for step in range(1, slides)]
+    enter(neighbours + others)
+
+    inner, ff = w_in_ref.shape
+    w_rows = (ff // channels) * inner
+    out_rows = w_out_ref.shape[0]
+    sources = [
+        (k * inner, inner, w_in_ref, w_in_sum, pl.ds(k * channels, channels))
+        for k in range(ff // channels)
+    ]
+    sources.append((w_rows, out_rows, w_out_ref, w_out_sum, slice(None)))
+    sources.append((w_rows + out_rows, rest_ref.shape[0], rest_ref, rest_sum, slice(None)))
+
+    def segments(low, high):
+        for first, length, given, summed, lanes in sources:
+            start, end = max(low, first), min(high, first + length)
+            if start < end:
+                yield pl.ds(start, end - start), pl.ds(start - first, end - start), given, summed, lanes
+
+    def sum_rows(low, high, index):
+        for here, there, given, _, lanes in segments(low, high):
+            total[here] = given[there, lanes]
+        rows = high - low
+        piece = rows // strips
+        part = piece // slides
+        size = rows // 2
+        starts = [low, low + size]
+        trail = []
+        box = low - low // strips
+        for stage in range(len(bits)):
+            size //= 2
+            copies = []
+            for half in range(2):
+                bit = orders[half][stage]
+                away = pl.multiple_of(starts[half] + (1 - mine[bit]) * size, 16)
+                outbox[pl.ds(box, size)] = total[pl.ds(away, size)].astype(outbox.dtype)
+                copies.append(
+                    send(
+                        outbox.at[pl.ds(box, size)],
+                        inbox.at[pl.ds(box, size)],
+                        send_sem,
+                        recv_sem,
+                        index,
+                        partner[bit],
+                    )
+                )
+                starts[half] = starts[half] + mine[bit] * size
+                box += size
+                index += 1
+            trail.append(size)
+            yield
+            for half in range(2):
+                copies[half].wait()
+                here = pl.ds(pl.multiple_of(starts[half], 16), size)
+                total[here] += inbox[pl.ds(box - (2 - half) * size, size)].astype(jnp.float32)
+
+        kept = [pl.ds(pl.multiple_of(starts[half], 16), size) for half in range(2)]
+        base = low // strips
+        for half in range(2):
+            slide_out[pl.ds(base + half * size, size)] = total[kept[half]].astype(slide_out.dtype)
+        copies, landed = [], []
+        for step, peer in enumerate(others):
+            their = pl.multiple_of(base + peer["slide"] * part, 16)
+            landed.append(pl.ds(base // slides + step * (slide_in.shape[0] // (slides - 1)), part))
+            copies.append(
+                send(
+                    slide_out.at[pl.ds(their, part)],
+                    slide_in.at[landed[step]],
+                    send_sem,
+                    recv_sem,
+                    index,
+                    peer,
+                )
+            )
+            index += 1
+        yield
+        own = pl.ds(pl.multiple_of(base + slide * part, 16), part)
+        value = slide_out[own].astype(jnp.float32)
+        for step, copy in enumerate(copies):
+            copy.wait()
+            value += slide_in[landed[step]].astype(jnp.float32)
+        joint[own] = value.astype(joint.dtype)
+        copies = []
+        for peer in others:
+            copies.append(send(joint.at[own], joint.at[own], send_sem, recv_sem, index, peer))
+            index += 1
+        yield
+        for copy in copies:
+            copy.wait()
+        for half in range(2):
+            result[kept[half]] = joint[pl.ds(base + half * size, size)]
+
+        for stage in reversed(range(len(bits))):
+            size = trail[stage]
+            copies = []
+            for half in range(2):
+                bit = orders[half][stage]
+                here = pl.ds(pl.multiple_of(starts[half], 16), size)
+                copies.append(
+                    send(result.at[here], result.at[here], send_sem, recv_sem, index, partner[bit])
+                )
+                starts[half] = starts[half] - mine[bit] * size
+                index += 1
+            yield
+            for copy in copies:
+                copy.wait()
+        for here, there, _, summed, lanes in segments(low, high):
+            summed[there, lanes] = result[here].astype(jnp.float32)
+
+    each = 4 * len(bits) + 2 * (slides - 1)
+    running = [sum_rows(low, high, k * each) for k, (low, high) in enumerate(groups)]
+    rounds = 0
+    own_copies = []
+    while running:
+        left = []
+        for group in running:
+            try:
+                next(group)
+                left.append(group)
+            except StopIteration:
+                pass
+        running = left
+        if rounds == len(bits):
+            own_copies = [
+                send(own_ref, all_ref.at[me], own_send_sem, own_recv_sem, index, peer)
+                for index, peer in enumerate(neighbours)
+            ]
+            all_ref[me] = own_ref[...]
+        rounds += 1
+    for copy in own_copies:
+        copy.wait()
+
+
+def sum_grads(g_w_in, g_w_out, others, own):
+    strips, slides = lax.axis_size("strip"), lax.axis_size("slide")
+    channels = g_w_out.shape[1]
+    height, width = own.shape[:2]
+    flat = [other.reshape(-1, channels) for other in others]
+    unit = strips * slides * 16
+    w_rows = g_w_in.size // channels + g_w_out.shape[0]
+    used = w_rows + sum(other.shape[0] for other in flat)
+    units = -(-used // unit)
+    rows = units * unit
+    if rows > used:
+        flat.append(jnp.zeros((rows - used, channels), jnp.float32))
+    rest = jnp.concatenate(flat, axis=0)
+    parts = min(units, 3)
+    edges = [-(-units * k // parts) * unit for k in range(parts + 1)]
+    groups = tuple(zip(edges[:-1], edges[1:]))
+    stages = strips.bit_length() - 1
+    count = parts * (4 * stages + 2 * (slides - 1))
+    piece = rows // strips
+    small = jnp.bfloat16
+    w_in_sum, w_out_sum, rest_sum, region = pl.pallas_call(
+        functools.partial(sum_kernel, strips, slides, groups),
+        out_shape=[
+            jax.ShapeDtypeStruct(g_w_in.shape, jnp.float32),
+            jax.ShapeDtypeStruct(g_w_out.shape, jnp.float32),
+            jax.ShapeDtypeStruct(rest.shape, jnp.float32),
+            jax.ShapeDtypeStruct((strips, height * width, channels), own.dtype),
+        ],
+        in_specs=[pl.BlockSpec(memory_space=pltpu.VMEM)] * 4,
+        out_specs=[pl.BlockSpec(memory_space=pltpu.VMEM)] * 4,
+        scratch_shapes=[
+            pltpu.VMEM((rows, channels), jnp.float32),
+            pltpu.VMEM((rows - piece, channels), small),
+            pltpu.VMEM((rows - piece, channels), small),
+            pltpu.VMEM((piece, channels), small),
+            pltpu.VMEM(((slides - 1) * (piece // slides), channels), small),
+            pltpu.VMEM((piece, channels), small),
+            pltpu.VMEM((rows, channels), small),
+            pltpu.SemaphoreType.DMA((count,)),
+            pltpu.SemaphoreType.DMA((count,)),
+            pltpu.SemaphoreType.DMA((strips - 1,)),
+            pltpu.SemaphoreType.DMA((strips - 1,)),
+        ],
+        compiler_params=pltpu.CompilerParams(
+            collective_id=3, has_side_effects=True, vmem_limit_bytes=vmem_bytes
+        ),
+    )(g_w_in, g_w_out, rest, own.reshape(height * width, channels))
+    summed, at = [], 0
+    for other in others:
+        length = other.size // channels
+        summed.append(rest_sum[at : at + length].reshape(other.shape))
+        at += length
+    return w_in_sum, w_out_sum, summed, region.reshape(strips * height, width, channels)
+
+
+def rows_around(region, margin, side, rows):
+    padded = jnp.pad(region, ((margin, margin), (side, side), (0, 0)))
+    start = lax.axis_index("strip") * rows
+    return lax.dynamic_slice_in_dim(padded, start, rows + 2 * margin, axis=0)
 
 
 def depth_conv(source, kernel, pad_rows, pad_cols):
@@ -49,31 +347,6 @@
         feature_group_count=padded.shape[-1],
         preferred_element_type=jnp.float32,
     )[0]
-
-
-def to_columns(source, rim_width):
-    turned = jax.tree.map(
-        lambda part, own: part.astype(own.dtype),
-        lax.all_to_all(for_sending(source), "strip", split_axis=1, concat_axis=0, tiled=True),
-        source,
-    )
-    return padded_2(for_sending(turned), (("strip", 1),), rim_width).astype(turned.dtype)
-
-
-def to_rows(source):
-    return jax.tree.map(
-        lambda part, own: part.astype(own.dtype),
-        lax.all_to_all(for_sending(source), "strip", split_axis=0, concat_axis=1, tiled=True),
-        source,
-    )
-
-
-def row_rims(source, rim_width):
-    return padded_2(for_sending(source), (("strip", 0),), rim_width).astype(source.dtype)
-
-
-def rows_margin(source, rim_width):
-    return row_rims(to_rows(source), rim_width)
 
 
 def local(
@@ -97,10 +370,19 @@
     scale_multiplier = jnp.float32(
         row_count * full_width * lax.axis_size("slide") * lax.axis_size("strip")
     ) ** (-0.5)
-    tall_cols = to_columns(source, rim_width)
-    mixed_cols = depth_conv(tall_cols, kernel_tall, tall_pad, 0).astype(jnp.bfloat16)
-    mixed_rows = rows_margin(mixed_cols, rim_width)
-    conv_out = depth_conv(mixed_rows, kernel_wide, 0, wide_pad)
+    reach = min(wide_pad, full_width - 1)
+    near = kernel_wide[:, wide_pad - reach : wide_pad + reach + 1]
+    region_rows = row_count * lax.axis_size("strip")
+    window = rows_around(gather_rows(source, 0), tall_pad + rim_width, rim_width, row_count)
+    place = (
+        lax.axis_index("strip") * row_count
+        - rim_width
+        + lax.broadcasted_iota(jnp.int32, (row_count + 2 * rim_width, 1, 1), 0)
+    )
+    mixed_rows = jnp.where(
+        (place >= 0) & (place < region_rows), depth_conv(window, kernel_tall, 0, 0), 0.0
+    ).astype(jnp.bfloat16)
+    conv_out = depth_conv(mixed_rows, near, 0, reach)
     mean_removed = conv_out - jnp.mean(conv_out, axis=-1, keepdims=True)
     inverse_deviation = lax.rsqrt(
         jnp.mean(mean_removed * mean_removed, axis=-1, keepdims=True) + epsilon
@@ -138,29 +420,23 @@
             * jnp.mean(grad_standardized * standardized_input, axis=-1, keepdims=True)
         )
     ).astype(jnp.bfloat16)
-    d_conv_rims = row_rims(grad_depth_output, rim_width)
-    d_mixed = depth_conv(d_conv_rims, kernel_wide[::-1, ::-1], 0, wide_pad).astype(jnp.bfloat16)
-    g_wide = (
-        kernel_grad(jnp.pad(mixed_rows, ((0, 0), (wide_pad, wide_pad), (0, 0))), grad_depth_output)
+    d_conv_rims = add_rims(grad_depth_output, rim_width, 1)
+    d_mixed = depth_conv(d_conv_rims, near[::-1, ::-1], 0, reach).astype(jnp.bfloat16)
+    g_near = (
+        kernel_grad(jnp.pad(mixed_rows, ((0, 0), (reach, reach), (0, 0))), grad_depth_output)
         * scale_multiplier
     )
-    d_mixed_cols = to_columns(d_mixed, rim_width)
-    g_tall = (
-        kernel_grad(
-            jnp.pad(tall_cols, ((tall_pad, tall_pad), (0, 0), (0, 0))),
-            d_mixed_cols[:, rim_width:-rim_width],
-        )
-        * scale_multiplier
-    )
-    d_image_cols = depth_conv(d_mixed_cols, kernel_tall[::-1, ::-1], tall_pad, 0).astype(
-        jnp.bfloat16
-    )
-    d_image = to_rows(d_image_cols)
+    g_tall = kernel_grad(window[rim_width:-rim_width], d_mixed) * scale_multiplier
+    g_w_in, g_w_out, (g_tall, g_near, grad_norm_gain, g_shift, g_b_in, g_b_out), d_region = sum_grads(
+        g_w_in,
+        g_w_out,
+        (g_tall, g_near, grad_norm_gain, g_shift, g_b_in, g_b_out),
+        d_mixed,
+    )
+    d_mixed_window = rows_around(d_region, tall_pad, rim_width, row_count)
+    d_image = depth_conv(d_mixed_window, kernel_tall[::-1, ::-1], 0, 0).astype(jnp.bfloat16)
     grad_image = (upstream.astype(jnp.float32) + d_image.astype(jnp.float32)).astype(jnp.bfloat16)
-    g_tall, g_wide, grad_norm_gain, g_shift, g_w_in, g_b_in, g_w_out, g_b_out = lax.psum(
-        (g_tall, g_wide, grad_norm_gain, g_shift, g_w_in, g_b_in, g_w_out, g_b_out),
-        ("slide", "strip"),
-    )
+    g_wide = jnp.pad(g_near, ((0, 0), (wide_pad - reach, wide_pad - reach), (0, 0)))
     return (
         output[None],
         grad_image[None],

time: 244 us -> 103 us (0.42)
  waiting for transfers between devices: 97.1 us -> 0 us
  blocking collectives: 49.6 us -> 0 us
  Pallas kernels: 0 us -> 44.1 us
  starting transfers between devices: 32.6 us -> 0 us
  between operations: 14.5 us -> 1.13 us
  local copies, waits for them, and re-layouts: 14.3 us -> 24.9 us
  matrix products: 32.5 us -> 26.4 us
  other arithmetic: 2.04 us -> 6.11 us
    psum x1 -> x0, waiting for transfers between devices: 81.5 us -> none  [local(): lax.psum((g_tall, g_wide, grad_norm_gain, g_shift, g_w_in, g_b_in, g_w_ou...]
    pallas_call x0 -> x3, Pallas kernels: none -> 44.1 us  [the longest x1 30.7 us: sum_grads(): pl.pallas_call(functools.partial(sum_kernel, strips, slides, groups), out...]
    psum x1 -> x0, blocking collectives: 39.6 us -> none  [local(): lax.psum((g_tall, g_wide, grad_norm_gain, g_shift, g_w_in, g_b_in, g_w_ou...]
    ppermute x8 -> x0, starting transfers between devices: 17.7 us -> none  [the longest x4 12.3 us: padded_2(): lax.ppermute(tail, axis, [(i, (i + 1) % count) for i in range(ends)])]
    all_to_all x3 -> x0, starting transfers between devices: 14.9 us -> none  [the longest x2 9.39 us: to_rows(): lax.all_to_all(for_sending(source), 'strip', split_axis=0, concat_axis=1,...]
    all_to_all x3 -> x0, waiting for transfers between devices: 12.5 us -> none  [the longest x2 8.92 us: to_rows(): lax.all_to_all(for_sending(source), 'strip', split_axis=0, concat_axis=1,...]
    all_to_all x1 -> x0, blocking collectives: 9.99 us -> none  [to_columns(): lax.all_to_all(for_sending(source), 'strip', split_axis=1, concat_axis=0,...]
    conv_general_dilated x4, matrix products: 20.3 us -> 12.7 us  [depth_conv(): lax.conv_general_dilated(source[None], kernel[:, :, None, :], (1, 1), ((p...]
  transfers between devices with their start and end apart: 12 -> 0, of which waited for: 6 -> 0; matrix products, arithmetic and copies ran while one was open for 9% -> 0% of each run, Pallas kernels for 0% -> 0%
where the time goes in v1:
time: 103 us
  Pallas kernels  44.1 us (43%)
  matrix products  26.4 us (26%)
  local copies, waits for them, and re-layouts  24.9 us (24%)
  other arithmetic  6.11 us (6%)
  between operations  1.13 us (1%)
    pallas_call x1, Pallas kernels, sum_grads(): pl.pallas_call(functools.partial(sum_kernel, strips, slides, groups), out...  30.7 us
    conv_general_dilated x4, matrix products, depth_conv(): lax.conv_general_dilated(source[None], kernel[:, :, None, :], (1, 1), ((p...  12.7 us
    unnamed x90, local copies, waits for them, and re-layouts  12 us
    conv_general_dilated x2, matrix products, kernel_grad(): lax.conv_general_dilated(padded[None], upstream[:, :, None, :], (1, 1), '...  10.7 us
    pallas_call x1, Pallas kernels, gather_rows(): pl.pallas_call(functools.partial(gather_kernel, count), out_shape=jax.Sha...  9.23 us
    pallas_call x1, Pallas kernels, add_rims(): pl.pallas_call(functools.partial(rim_kernel, count, size), out_shape=jax....  4.12 us
    concatenate x1, local copies, waits for them, and re-layouts, sum_grads(): rest = jnp.concatenate(flat, axis=0)  2.65 us

profile of v1, /device:TPU:0, one launch (start us, length us, event | category | flops | bytes accessed | tf_op | source)
XLA Modules:
  0.0 102.6 jit_solution(16928273091040188619)
XLA Ops:
  0.7 1.6 %fusion.60 = (bf16[5,31,256]{2,1,0:T(8,128)(2,1)}, bf16[5,31,1,256]{3,1,0,2:T(8,128)(2,1)S(1)}) fusion(bf16[5,51,256]{2,1,0:T(8,128)(2,1)} %param.13), kind=kLoop, calls=%fused_computation.90 | loop fusion | bytes 238080 | tf_op jit(solution)/shard_map/slice | solution.py:374
  2.3 0.8 copy-done.7
  3.1 9.2 %shard_map.177 = bf16[8,96,256]{2,1,0:T(8,128)(2,1)S(1)} custom-call(bf16[96,256]{1,0:T(8,128)(2,1)S(1)} %bitcast.83), custom_call_target="tpu_custom_call" | custom-call | tf_op jit(solution)/shard_map/pallas_call | solution.py:51
  12.6 4.4 %fusion = bf16[1,10,16,256]{3,0,2,1:T(2,128)(2,1)S(1)} fusion(bf16[1,60,20,256]{3,1,2,0:T(8,128)(2,1)S(1)} %fusion.26, bf16[51,5,1,256]{3,0,1,2:T(8,128)(2,1)S(1)} %bitcast.89), kind=kOutput, calls=%fused_computation.4 | convolution fusion | flops 20889600 | bytes 826880 | tf_op jit(solution)/shard_map/conv_general_dilated | solution.py:329
  17.6 2.3 %fusion.61 = (f32[6,16]{1,0:T(8,128)S(1)}, f32[1,6,16,256]{3,0,2,1:T(1,128)S(1)}) fusion(bf16[5,31,1,256]{3,1,0,2:T(8,128)(2,1)S(1)} %get-tuple-element.46, bf16[1,10,16,256]{3,0,2,1:T(2,128)(2,1)S(1)} %fusion, pred[10]{0:T(512)(128)(4,1)S(1)} %compare_and_fusion), kind=kOutput, calls=%fused_computation.91 | convolution fusion | flops 3997600 | bytes 259978 | tf_op jit(solution)/shard_map/conv_general_dilated | solution.py:329
  22.8 0.9 convert_reduce_fusion
  25.1 1.0 fusion.28
  26.1 0.9 multiply_reduce_fusion
  27.6 4.1 %shard_map.178 = bf16[2,32,256]{2,1,0:T(8,128)(2,1)S(1)} custom-call(bf16[96,256]{1,0:T(8,128)(2,1)S(1)} %multiply_convert_fusion.2.own_ref), custom_call_target="tpu_custom_call" | custom-call | tf_op jit(solution)/shard_map/pallas_call | solution.py:86
  33.8 0.8 multiply_convert_fusion.1
  34.6 1.4 %maximum_bitcast_fusion = bf16[1,10,16,256]{3,2,1,0:T(8,128)(2,1)} fusion(bf16[2,16,256]{2,1,0:T(8,128)(2,1)} %bitcast.93, bf16[6,16,256]{2,1,0:T(8,128)(2,1)S(1)} %multiply_convert_fusion.1, bf16[2,16,256]{2,1,0:T(8,128)(2,1)} %bitcast.92), kind=kLoop, calls=%fused_computation.67 | loop fusion | flops 81920 | bytes 163840 | tf_op jit(solution)/shard_map/broadcast_in_dim | solution.py:330
  36.8 3.0 %convolution_convert_fusion = bf16[1,6,16,256]{3,0,2,1:T(2,128)(2,1)} fusion(bf16[1,10,16,256]{3,2,1,0:T(8,128)(2,1)} %maximum_bitcast_fusion, bf16[5,31,1,256]{3,1,0,2:T(8,128)(2,1)} %bitcast.91), kind=kOutput, calls=%fused_computation.16 | convolution fusion | flops 3956736 | bytes 210432 | tf_op jit(solution)/shard_map/conv_general_dilated | solution.py:329
  39.8 7.1 %fusion.16 = f32[51,5,256]{2,1,0:T(8,128)} fusion(bf16[1,56,20,256]{3,1,2,0:T(8,128)(2,1)S(1)} %copy-done.11, bf16[1,6,16,256]{3,0,2,1:T(2,128)(2,1)} %convolution_convert_fusion), kind=kOutput, calls=%fused_computation.18 | convolution fusion | flops 12599040 | bytes 883712 | tf_op jit(solution)/shard_map/conv_general_dilated | solution.py:341
  46.8 1.1 %mul.276 = f32[255,256]{1,0:T(8,128)S(1)} reshape(f32[51,5,256]{2,1,0:T(8,128)} %fusion.16) | data formatting | bytes 522240 | tf_op jit(solution)/shard_map/mul | solution.py:429
  47.9 1.0 fusion.36
  49.7 3.7 %fusion.19 = f32[5,31,256]{2,1,0:T(8,128)S(1)} fusion(bf16[1,10,46,256]{3,2,1,0:T(8,128)(2,1)S(1)} %pad_bitcast_fusion, f32[1,6,16,256]{3,0,2,1:T(1,128)S(1)} %get-tuple-element.50, f32[6,16,1,256]{3,2,1,0:T(1,128)} %reshape.245, f32[6,16]{1,0:T(8,128)} %copy-done.22, f32[6,16]{1,0:T(8,128)S(1)} %copy-done.19, f32[6,16]{1,0:T(8,128)} %copy-done.23, ...), kind=kOutput, calls=%fused_computation.20 | convolution fusion | flops 7854848 | bytes 593408 | tf_op jit(solution)/shard_map/conv_general_dilated | solution.py:341
  56.0 2.6 %concatenate.7.rest_ref = f32[512,256]{1,0:T(8,128)S(1)} concatenate(f32[255,256]{1,0:T(8,128)S(1)} %mul.276, f32[155,256]{1,0:T(8,128)} %mul.286, f32[1,256]{1,0:T(1,128)} %bitcast.96, f32[1,256]{1,0:T(1,128)} %bitcast.95, f32[4,256]{1,0:T(4,128)} %mul.295, f32[1,256]{1,0:T(1,128)} %bitcast.94, f32[95,256]{1,0:T(8,128)S(1)} %broadcast_in_dim.77), dimensions={0} | concatenate | bytes 1048576 | tf_op jit(solution)/shard_map/concatenate | solution.py:279
  58.7 0.9 copy.49
  59.6 30.7 %shard_map.179 = (f32[256,1024]{1,0:T(8,128)S(1)}, f32[1024,256]{1,0:T(8,128)S(1)}, f32[512,256]{1,0:T(8,128)S(1)}, bf16[8,96,256]{2,1,0:T(8,128)(2,1)S(1)}) custom-call(f32[256,1024]{1,0:T(8,128)S(1)} %convolution_multiply_fusion.1.w_in_ref, f32[1024,256]{1,0:T(8,128)S(1)} %convolution_multiply_fusion.w_out_ref, f32[512,256]{1,0:T(8,128)S(1)} %concatenate.7.rest_ref, ...), custom_call_target="tpu_custom_call" | custom-call | tf_op jit(solution)/shard_map/pallas_call | solution.py:287
  90.3 1.0 copy-done.1
  91.3 1.0 copy-done.3
  93.5 3.0 %fusion.23 = bf16[1,6,16,256]{3,0,2,1:T(2,128)(2,1)S(1)} fusion(bf16[1,56,20,256]{3,1,2,0:T(8,128)(2,1)S(1)} %fusion.27, bf16[51,5,1,256]{3,0,1,2:T(8,128)(2,1)S(1)} %bitcast.90, bf16[1,6,16,256]{3,2,1,0:T(8,128)(2,1)S(1)} %copy-done.14), kind=kOutput, calls=%fused_computation.22 | convolution fusion | flops 12656640 | bytes 802304 | tf_op jit(solution)/shard_map/conv_general_dilated | solution.py:329
  100.0 1.0 copy.93
  101.6 1.0 copy.94
  (122 shorter events, 17.1 us)
Async XLA Ops:
  0.6 20.8 %copy-start = (bf16[256,1024]{1,0:T(8,128)(2,1)S(1)}, bf16[256,1024]{1,0:T(8,128)(2,1)}, u32[]{:S(2)}) copy-start(bf16[256,1024]{1,0:T(8,128)(2,1)} %param.16) | copy-start | bytes 1572868
  3.1 9.6 %copy-start.16 = (bf16[51,5,256]{2,0,1:T(8,128)(2,1)S(1)}, bf16[51,5,256]{2,0,1:T(8,128)(2,1)}, u32[]{:S(2)}) copy-start(bf16[51,5,256]{2,0,1:T(8,128)(2,1)} %param.12) | copy-start | bytes 391684
  17.0 3.4 %copy-start.15 = (bf16[1,10,16,256]{3,0,2,1:T(2,128)(2,1)}, bf16[1,10,16,256]{3,0,2,1:T(2,128)(2,1)S(1)}, u32[]{:S(2)}) copy-start(bf16[1,10,16,256]{3,0,2,1:T(2,128)(2,1)S(1)} %fusion) | copy-start | bytes 245764
  17.6 3.7 %copy-start.24 = (f32[256]{0:T(256)S(1)}, f32[256]{0:T(256)}, u32[]{:S(2)}) copy-start(f32[256]{0:T(256)} %param.14) | copy-start | bytes 3076
  17.6 3.7 %copy-start.37 = (f32[256]{0:T(256)S(1)}, f32[256]{0:T(256)}, u32[]{:S(2)}) copy-start(f32[256]{0:T(256)} %param.15) | copy-start | bytes 3076
  17.6 3.8 %copy-start.33 = (f32[1024]{0:T(1024)S(1)}, f32[1024]{0:T(1024)}, u32[]{:S(2)}) copy-start(f32[1024]{0:T(1024)} %param.17) | copy-start | bytes 12292
  20.0 1.8 %copy-start.12 = (bf16[1024,256]{1,0:T(8,128)(2,1)S(1)}, bf16[1024,256]{1,0:T(8,128)(2,1)}, u32[]{:S(2)}) copy-start(bf16[1024,256]{1,0:T(8,128)(2,1)} %param.18) | copy-start | bytes 1572868
  20.0 1.8 %copy-start.38 = (f32[256]{0:T(256)S(1)}, f32[256]{0:T(256)}, u32[]{:S(2)}) copy-start(f32[256]{0:T(256)} %param.19) | copy-start | bytes 3076
  24.7 1.4 %copy-start.25 = (f32[256]{0:T(256)S(1)}, f32[256]{0:T(256)}, u32[]{:S(2)}) copy-start(f32[256]{0:T(256)} %param.14) | copy-start | bytes 3076
  24.7 1.4 %copy-start.28 = (f32[96]{0:T(128)S(1)}, f32[96]{0:T(128)}, u32[]{:S(2)}) copy-start(f32[96]{0:T(128)} %copy-done.27) | copy-start | bytes 1156
  26.0 10.0 %copy-start.13 = (bf16[5,31,256]{2,1,0:T(8,128)(2,1)S(1)}, bf16[5,31,256]{2,1,0:T(8,128)(2,1)}, u32[]{:S(2)}) copy-start(bf16[5,31,256]{2,1,0:T(8,128)(2,1)} %get-tuple-element.45) | copy-start | bytes 238084
  27.6 12.2 %copy-start.11 = (bf16[1,56,20,256]{3,1,2,0:T(8,128)(2,1)S(1)}, bf16[1,56,20,256]{3,1,2,0:T(8,128)(2,1)}, u32[]{:S(2)}) copy-start(bf16[1,56,20,256]{3,1,2,0:T(8,128)(2,1)} %fusion.28) | copy-start | bytes 1720324
  33.1 13.7 %copy-start.22 = (f32[6,16]{1,0:T(8,128)}, f32[6,16]{1,0:T(8,128)S(1)}, u32[]{:S(2)}) copy-start(f32[6,16]{1,0:T(8,128)S(1)} %div.24) | copy-start | bytes 1156
  33.8 13.0 %copy-start.23 = (f32[6,16]{1,0:T(8,128)}, f32[6,16]{1,0:T(8,128)S(1)}, u32[]{:S(2)}) copy-start(f32[6,16]{1,0:T(8,128)S(1)} %div.23) | copy-start | bytes 1156
  39.8 8.1 %copy-start.40 = (pred[10]{0:T(512)(128)(4,1)S(1)}, pred[10]{0:T(512)(128)(4,1)}, u32[]{:S(2)}) copy-start(pred[10]{0:T(512)(128)(4,1)} %copy-done.39) | copy-start | bytes 34
  46.8 2.9 %copy-start.19 = (f32[6,16]{1,0:T(8,128)S(1)}, f32[6,16]{1,0:T(8,128)}, u32[]{:S(2)}) copy-start(f32[6,16]{1,0:T(8,128)} %copy-done.18) | copy-start | bytes 1156
  46.8 2.9 %copy-start.21 = (f32[6,16]{1,0:T(8,128)S(1)}, f32[6,16]{1,0:T(8,128)}, u32[]{:S(2)}) copy-start(f32[6,16]{1,0:T(8,128)} %copy-done.20) | copy-start | bytes 1156
  46.8 2.9 %copy-start.26 = (f32[256]{0:T(256)S(1)}, f32[256]{0:T(256)}, u32[]{:S(2)}) copy-start(f32[256]{0:T(256)} %param.14) | copy-start | bytes 3076
  49.7 4.4 %copy-start.35 = (f32[256]{0:T(256)S(1)}, f32[256]{0:T(256)}, u32[]{:S(2)}) copy-start(f32[256]{0:T(256)} %get-tuple-element.38) | copy-start | bytes 3076
  49.7 4.4 %copy-start.36 = (f32[256]{0:T(256)S(1)}, f32[256]{0:T(256)}, u32[]{:S(2)}) copy-start(f32[256]{0:T(256)} %get-tuple-element.41) | copy-start | bytes 3076
  49.7 5.0 %copy-start.34 = (f32[1024]{0:T(1024)S(1)}, f32[1024]{0:T(1024)}, u32[]{:S(2)}) copy-start(f32[1024]{0:T(1024)} %get-tuple-element.54) | copy-start | bytes 12292
  93.5 3.7 %copy-start.6 = (f32[512,256]{1,0:T(8,128)S(1)}, f32[512,256]{1,0:T(8,128)}, u32[]{:S(2)}) copy-start(f32[512,256]{1,0:T(8,128)} %copy-done.5) | copy-start | bytes 1572868
  97.3 2.8 %copy-start.4 = (f32[256,1024]{1,0:T(8,128)S(1)}, f32[256,1024]{1,0:T(8,128)}, u32[]{:S(2)}) copy-start(f32[256,1024]{1,0:T(8,128)} %copy-done.3) | copy-start | bytes 3145732
  100.0 1.6 %copy-start.2 = (f32[1024,256]{1,0:T(8,128)S(1)}, f32[1024,256]{1,0:T(8,128)}, u32[]{:S(2)}) copy-start(f32[1024,256]{1,0:T(8,128)} %copy-done.1) | copy-start | bytes 3145732
  (17 other events, 13.5 us)

commit v2 on v1

--- a/solution.py
+++ b/solution.py
@@ -1,4 +1,5 @@
 import functools
+import math
 
 import jax
 import jax.numpy as jnp
@@ -8,8 +9,11 @@
 from jax.sharding import PartitionSpec as P
 
 epsilon = 1e-06
-vmem_bytes = 48 * 1024 * 1024
 MESH = pl.DeviceIdType.MESH
+
+
+def vmem_for(*arrays):
+    return 4 * 1024 * 1024 + sum(math.prod(shape) * width for shape, width in arrays)
 
 
 def enter(peers):
@@ -58,7 +62,9 @@
             pltpu.SemaphoreType.DMA((count - 1,)),
         ],
         compiler_params=pltpu.CompilerParams(
-            collective_id=collective_id, has_side_effects=True, vmem_limit_bytes=vmem_bytes
+            collective_id=collective_id,
+            has_side_effects=True,
+            vmem_limit_bytes=vmem_for((own.shape, 2), ((count, *own.shape), 2)),
         ),
     )(own.reshape(rows * width, channels))
     return gathered.reshape(count * rows, width, channels)
@@ -90,7 +96,9 @@
         out_specs=pl.BlockSpec(memory_space=pltpu.VMEM),
         scratch_shapes=[pltpu.SemaphoreType.DMA((2,)), pltpu.SemaphoreType.DMA((2,))],
         compiler_params=pltpu.CompilerParams(
-            collective_id=collective_id, has_side_effects=True, vmem_limit_bytes=vmem_bytes
+            collective_id=collective_id,
+            has_side_effects=True,
+            vmem_limit_bytes=vmem_for((own.shape, 2), ((2, size, channels), 2)),
         ),
     )(own.reshape(rows * width, channels))
     rims = rims.reshape(2, rim_width, width, channels)
@@ -308,7 +316,14 @@
             pltpu.SemaphoreType.DMA((strips - 1,)),
         ],
         compiler_params=pltpu.CompilerParams(
-            collective_id=3, has_side_effects=True, vmem_limit_bytes=vmem_bytes
+            collective_id=3,
+            has_side_effects=True,
+            vmem_limit_bytes=vmem_for(
+                ((3, rows, channels), 4),
+                ((3, rows, channels), 2),
+                ((3, piece, channels), 2),
+                ((strips + 1, *own.shape), 2),
+            ),
         ),
     )(g_w_in, g_w_out, rest, own.reshape(height * width, channels))
     summed, at = [], 0
@@ -426,7 +441,12 @@
         kernel_grad(jnp.pad(mixed_rows, ((0, 0), (reach, reach), (0, 0))), grad_depth_output)
         * scale_multiplier
     )
-    g_tall = kernel_grad(window[rim_width:-rim_width], d_mixed) * scale_multiplier
+    g_tall = (
+        kernel_grad(
+            jnp.swapaxes(window[rim_width:-rim_width], 0, 1), jnp.swapaxes(d_mixed, 0, 1)
+        )
+        * scale_multiplier
+    )
     g_w_in, g_w_out, (g_tall, g_near, grad_norm_gain, g_shift, g_b_in, g_b_out), d_region = sum_grads(
         g_w_in,
         g_w_out,
@@ -437,6 +457,7 @@
     d_image = depth_conv(d_mixed_window, kernel_tall[::-1, ::-1], 0, 0).astype(jnp.bfloat16)
     grad_image = (upstream.astype(jnp.float32) + d_image.astype(jnp.float32)).astype(jnp.bfloat16)
     g_wide = jnp.pad(g_near, ((0, 0), (wide_pad - reach, wide_pad - reach), (0, 0)))
+    g_tall = jnp.swapaxes(g_tall, 0, 1)
     return (
         output[None],
         grad_image[None],

time: 103 us -> 102 us (level)
  matrix products: 26.4 us -> 23.3 us
  local copies, waits for them, and re-layouts: 24.9 us -> 26.2 us
    conv_general_dilated x2, matrix products: 10.7 us -> 8.21 us  [kernel_grad(): lax.conv_general_dilated(padded[None], upstream[:, :, None, :], (1, 1), '...]
    unnamed x90 -> x94, local copies, waits for them, and re-layouts: 12 us -> 11 us
where the time goes in v2:
time: 102 us; the launch traced here: 101 us
  Pallas kernels  44.1 us (43%)
  local copies, waits for them, and re-layouts  26.2 us (26%)
  matrix products  23.3 us (23%)
  other arithmetic  6.11 us (6%)
  between operations  1.16 us (1%)
    pallas_call x1, Pallas kernels, sum_grads(): pl.pallas_call(functools.partial(sum_kernel, strips, slides, groups), out...  30.7 us
    conv_general_dilated x4, matrix products, depth_conv(): lax.conv_general_dilated(source[None], kernel[:, :, None, :], (1, 1), ((p...  12.1 us
    unnamed x94, local copies, waits for them, and re-layouts  11 us
    pallas_call x1, Pallas kernels, gather_rows(): pl.pallas_call(functools.partial(gather_kernel, count), out_shape=jax.Sha...  9.23 us
    conv_general_dilated x2, matrix products, kernel_grad(): lax.conv_general_dilated(padded[None], upstream[:, :, None, :], (1, 1), '...  8.21 us
    pallas_call x1, Pallas kernels, add_rims(): pl.pallas_call(functools.partial(rim_kernel, count, size), out_shape=jax....  4.12 us
    concatenate x1, local copies, waits for them, and re-layouts, sum_grads(): rest = jnp.concatenate(flat, axis=0)  3.57 us

profile of v2, /device:TPU:0, one launch (start us, length us, event | category | flops | bytes accessed | tf_op | source)
XLA Modules:
  0.0 100.8 jit_solution(1170821701106223014)
XLA Ops:
  0.7 1.6 %fusion.60 = (bf16[5,31,256]{2,1,0:T(8,128)(2,1)}, bf16[5,31,1,256]{3,1,0,2:T(8,128)(2,1)S(1)}) fusion(bf16[5,51,256]{2,1,0:T(8,128)(2,1)} %param.13), kind=kLoop, calls=%fused_computation.90 | loop fusion | bytes 238080 | tf_op jit(solution)/shard_map/slice | solution.py:389
  2.3 0.8 copy-done.7
  3.1 9.2 %shard_map.177 = bf16[8,96,256]{2,1,0:T(8,128)(2,1)S(1)} custom-call(bf16[96,256]{1,0:T(8,128)(2,1)S(1)} %bitcast.90), custom_call_target="tpu_custom_call" | custom-call | tf_op jit(solution)/shard_map/pallas_call | solution.py:55
  12.6 4.4 %fusion = bf16[1,10,16,256]{3,0,2,1:T(2,128)(2,1)S(1)} fusion(bf16[1,60,20,256]{3,1,2,0:T(8,128)(2,1)S(1)} %fusion.26, bf16[51,5,1,256]{3,0,1,2:T(8,128)(2,1)S(1)} %bitcast.97), kind=kOutput, calls=%fused_computation.4 | convolution fusion | flops 20889600 | bytes 826880 | tf_op jit(solution)/shard_map/conv_general_dilated | solution.py:344
  17.7 2.3 %fusion.61 = (f32[6,16]{1,0:T(8,128)S(1)}, f32[1,6,16,256]{3,0,2,1:T(1,128)S(1)}) fusion(bf16[5,31,1,256]{3,1,0,2:T(8,128)(2,1)S(1)} %get-tuple-element.46, bf16[1,10,16,256]{3,0,2,1:T(2,128)(2,1)S(1)} %fusion, pred[10]{0:T(512)(128)(4,1)S(1)} %compare_and_fusion), kind=kOutput, calls=%fused_computation.91 | convolution fusion | flops 3997600 | bytes 259978 | tf_op jit(solution)/shard_map/conv_general_dilated | solution.py:344
  22.8 0.9 convert_reduce_fusion
  25.1 1.0 fusion.28
  26.1 0.9 multiply_reduce_fusion
  27.6 4.1 %shard_map.178 = bf16[2,32,256]{2,1,0:T(8,128)(2,1)S(1)} custom-call(bf16[96,256]{1,0:T(8,128)(2,1)S(1)} %multiply_convert_fusion.2.own_ref), custom_call_target="tpu_custom_call" | custom-call | tf_op jit(solution)/shard_map/pallas_call | solution.py:92
  32.4 0.8 div.24
  33.9 0.8 multiply_convert_fusion.1
  34.7 1.4 %maximum_bitcast_fusion = bf16[1,10,16,256]{3,2,1,0:T(8,128)(2,1)} fusion(bf16[2,16,256]{2,1,0:T(8,128)(2,1)} %bitcast.101, bf16[6,16,256]{2,1,0:T(8,128)(2,1)S(1)} %multiply_convert_fusion.1, bf16[2,16,256]{2,1,0:T(8,128)(2,1)} %bitcast.100), kind=kLoop, calls=%fused_computation.67 | loop fusion | flops 81920 | bytes 163840 | tf_op jit(solution)/shard_map/broadcast_in_dim | solution.py:345
  36.9 2.4 %convolution_convert_fusion = bf16[1,6,16,256]{3,0,2,1:T(2,128)(2,1)S(1)} fusion(bf16[1,10,16,256]{3,2,1,0:T(8,128)(2,1)} %maximum_bitcast_fusion, bf16[5,31,1,256]{3,1,0,2:T(8,128)(2,1)} %bitcast.99), kind=kOutput, calls=%fused_computation.16 | convolution fusion | flops 3956736 | bytes 210432 | tf_op jit(solution)/shard_map/conv_general_dilated | solution.py:344
  39.9 4.5 %fusion.16 = f32[5,51,256]{2,1,0:T(8,128)} fusion(bf16[1,20,56,256]{3,2,1,0:T(8,128)(2,1)S(1)} %copy-done.11, bf16[16,6,1,256]{3,0,1,2:T(8,128)(2,1)S(1)} %bitcast.102), kind=kOutput, calls=%fused_computation.18 | convolution fusion | flops 12599040 | bytes 883712 | tf_op jit(solution)/shard_map/conv_general_dilated | solution.py:356
  44.5 1.0 mul.276
  45.5 1.0 fusion.36
  47.3 3.7 %fusion.19 = f32[5,31,256]{2,1,0:T(8,128)S(1)} fusion(bf16[1,10,46,256]{3,2,1,0:T(8,128)(2,1)S(1)} %pad_bitcast_fusion, f32[1,6,16,256]{3,0,2,1:T(1,128)S(1)} %get-tuple-element.50, f32[6,16,1,256]{3,2,1,0:T(1,128)} %reshape.235, f32[6,16]{1,0:T(8,128)} %copy-done.24, f32[6,16]{1,0:T(8,128)S(1)} %copy-done.21, f32[6,16]{1,0:T(8,128)} %copy-done.25, ...), kind=kOutput, calls=%fused_computation.20 | convolution fusion | flops 7854848 | bytes 593408 | tf_op jit(solution)/shard_map/conv_general_dilated | solution.py:356
  54.2 3.6 %concatenate.7.rest_ref = f32[512,256]{1,0:T(8,128)S(1)} concatenate(f32[255,256]{1,0:T(8,128)S(1)} %mul.276, f32[155,256]{1,0:T(8,128)} %mul.286, f32[1,256]{1,0:T(1,128)} %bitcast.105, f32[1,256]{1,0:T(1,128)} %bitcast.104, f32[4,256]{1,0:T(4,128)} %mul.295, f32[1,256]{1,0:T(1,128)} %bitcast.103, f32[95,256]{1,0:T(8,128)} %broadcast_in_dim.80), dimensions={0} | concatenate | bytes 1048576 | tf_op jit(solution)/shard_map/concatenate | solution.py:287
  57.9 30.7 %shard_map.179 = (f32[256,1024]{1,0:T(8,128)S(1)}, f32[1024,256]{1,0:T(8,128)S(1)}, f32[512,256]{1,0:T(8,128)S(1)}, bf16[8,96,256]{2,1,0:T(8,128)(2,1)S(1)}) custom-call(f32[256,1024]{1,0:T(8,128)S(1)} %convolution_multiply_fusion.1.w_in_ref, f32[1024,256]{1,0:T(8,128)S(1)} %convolution_multiply_fusion.w_out_ref, f32[512,256]{1,0:T(8,128)S(1)} %concatenate.7.rest_ref, ...), custom_call_target="tpu_custom_call" | custom-call | tf_op jit(solution)/shard_map/pallas_call | solution.py:295
  88.6 1.0 copy-done.1
  89.6 1.0 copy-done.3
  91.8 3.0 %fusion.23 = bf16[1,6,16,256]{3,0,2,1:T(2,128)(2,1)S(1)} fusion(bf16[1,56,20,256]{3,1,2,0:T(8,128)(2,1)S(1)} %fusion.27, bf16[51,5,1,256]{3,0,1,2:T(8,128)(2,1)S(1)} %bitcast.98, bf16[1,6,16,256]{3,2,1,0:T(8,128)(2,1)S(1)} %copy-done.16), kind=kOutput, calls=%fused_computation.22 | convolution fusion | flops 12656640 | bytes 802304 | tf_op jit(solution)/shard_map/conv_general_dilated | solution.py:344
  98.2 1.0 copy.98
  99.8 1.0 copy.99
  (126 shorter events, 17.6 us)
Async XLA Ops:
  0.6 20.8 %copy-start = (bf16[256,1024]{1,0:T(8,128)(2,1)S(1)}, bf16[256,1024]{1,0:T(8,128)(2,1)}, u32[]{:S(2)}) copy-start(bf16[256,1024]{1,0:T(8,128)(2,1)} %param.16) | copy-start | bytes 1572868
  3.1 9.6 %copy-start.18 = (bf16[51,5,256]{2,0,1:T(8,128)(2,1)S(1)}, bf16[51,5,256]{2,0,1:T(8,128)(2,1)}, u32[]{:S(2)}) copy-start(bf16[51,5,256]{2,0,1:T(8,128)(2,1)} %param.12) | copy-start | bytes 391684
  17.0 3.4 %copy-start.17 = (bf16[1,10,16,256]{3,0,2,1:T(2,128)(2,1)}, bf16[1,10,16,256]{3,0,2,1:T(2,128)(2,1)S(1)}, u32[]{:S(2)}) copy-start(bf16[1,10,16,256]{3,0,2,1:T(2,128)(2,1)S(1)} %fusion) | copy-start | bytes 245764
  17.7 3.7 %copy-start.26 = (f32[256]{0:T(256)S(1)}, f32[256]{0:T(256)}, u32[]{:S(2)}) copy-start(f32[256]{0:T(256)} %param.14) | copy-start | bytes 3076
  17.7 3.7 %copy-start.39 = (f32[256]{0:T(256)S(1)}, f32[256]{0:T(256)}, u32[]{:S(2)}) copy-start(f32[256]{0:T(256)} %param.15) | copy-start | bytes 3076
  17.7 3.8 %copy-start.35 = (f32[1024]{0:T(1024)S(1)}, f32[1024]{0:T(1024)}, u32[]{:S(2)}) copy-start(f32[1024]{0:T(1024)} %param.17) | copy-start | bytes 12292
  20.0 1.8 %copy-start.12 = (bf16[1024,256]{1,0:T(8,128)(2,1)S(1)}, bf16[1024,256]{1,0:T(8,128)(2,1)}, u32[]{:S(2)}) copy-start(bf16[1024,256]{1,0:T(8,128)(2,1)} %param.18) | copy-start | bytes 1572868
  20.0 1.8 %copy-start.40 = (f32[256]{0:T(256)S(1)}, f32[256]{0:T(256)}, u32[]{:S(2)}) copy-start(f32[256]{0:T(256)} %param.19) | copy-start | bytes 3076
  26.1 10.0 %copy-start.15 = (bf16[5,31,256]{2,1,0:T(8,128)(2,1)S(1)}, bf16[5,31,256]{2,1,0:T(8,128)(2,1)}, u32[]{:S(2)}) copy-start(bf16[5,31,256]{2,1,0:T(8,128)(2,1)} %get-tuple-element.45) | copy-start | bytes 238084
  27.0 4.8 %copy-start.33 = (f32[96]{0:T(128)}, f32[96]{0:T(128)S(1)}, u32[]{:S(2)}) copy-start(f32[96]{0:T(128)S(1)} %get-tuple-element.59) | copy-start | bytes 1156
  32.4 7.5 %copy-start.11 = (bf16[1,20,56,256]{3,2,1,0:T(8,128)(2,1)S(1)}, bf16[1,20,56,256]{3,2,1,0:T(8,128)(2,1)}, u32[]{:S(2)}) copy-start(bf16[1,20,56,256]{3,2,1,0:T(8,128)(2,1)} %fusion.28) | copy-start | bytes 1720324
  33.2 11.3 %copy-start.24 = (f32[6,16]{1,0:T(8,128)}, f32[6,16]{1,0:T(8,128)S(1)}, u32[]{:S(2)}) copy-start(f32[6,16]{1,0:T(8,128)S(1)} %div.24) | copy-start | bytes 1156
  33.9 10.6 %copy-start.25 = (f32[6,16]{1,0:T(8,128)}, f32[6,16]{1,0:T(8,128)S(1)}, u32[]{:S(2)}) copy-start(f32[6,16]{1,0:T(8,128)S(1)} %div.23) | copy-start | bytes 1156
  39.9 5.6 %copy-start.42 = (pred[10]{0:T(512)(128)(4,1)S(1)}, pred[10]{0:T(512)(128)(4,1)}, u32[]{:S(2)}) copy-start(pred[10]{0:T(512)(128)(4,1)} %copy-done.41) | copy-start | bytes 34
  44.5 2.8 %copy-start.21 = (f32[6,16]{1,0:T(8,128)S(1)}, f32[6,16]{1,0:T(8,128)}, u32[]{:S(2)}) copy-start(f32[6,16]{1,0:T(8,128)} %copy-done.20) | copy-start | bytes 1156
  44.5 2.8 %copy-start.23 = (f32[6,16]{1,0:T(8,128)S(1)}, f32[6,16]{1,0:T(8,128)}, u32[]{:S(2)}) copy-start(f32[6,16]{1,0:T(8,128)} %copy-done.22) | copy-start | bytes 1156
  44.5 2.8 %copy-start.28 = (f32[256]{0:T(256)S(1)}, f32[256]{0:T(256)}, u32[]{:S(2)}) copy-start(f32[256]{0:T(256)} %param.14) | copy-start | bytes 3076
  47.3 4.4 %copy-start.37 = (f32[256]{0:T(256)S(1)}, f32[256]{0:T(256)}, u32[]{:S(2)}) copy-start(f32[256]{0:T(256)} %get-tuple-element.38) | copy-start | bytes 3076
  47.3 4.4 %copy-start.38 = (f32[256]{0:T(256)S(1)}, f32[256]{0:T(256)}, u32[]{:S(2)}) copy-start(f32[256]{0:T(256)} %get-tuple-element.41) | copy-start | bytes 3076
  47.3 5.0 %copy-start.36 = (f32[1024]{0:T(1024)S(1)}, f32[1024]{0:T(1024)}, u32[]{:S(2)}) copy-start(f32[1024]{0:T(1024)} %get-tuple-element.54) | copy-start | bytes 12292
  51.0 6.8 %copy-start.14 = (bf16[1,6,16,256]{3,0,2,1:T(2,128)(2,1)S(1)}, bf16[1,6,16,256]{3,0,2,1:T(2,128)(2,1)}, u32[]{:S(2)}) copy-start(bf16[1,6,16,256]{3,0,2,1:T(2,128)(2,1)} %copy-done.13) | copy-start | bytes 147460
  91.8 3.7 %copy-start.6 = (f32[512,256]{1,0:T(8,128)S(1)}, f32[512,256]{1,0:T(8,128)}, u32[]{:S(2)}) copy-start(f32[512,256]{1,0:T(8,128)} %copy-done.5) | copy-start | bytes 1572868
  95.5 2.7 %copy-start.4 = (f32[256,1024]{1,0:T(8,128)S(1)}, f32[256,1024]{1,0:T(8,128)}, u32[]{:S(2)}) copy-start(f32[256,1024]{1,0:T(8,128)} %copy-done.3) | copy-start | bytes 3145732
  98.2 1.6 %copy-start.2 = (f32[1024,256]{1,0:T(8,128)S(1)}, f32[1024,256]{1,0:T(8,128)}, u32[]{:S(2)}) copy-start(f32[1024,256]{1,0:T(8,128)} %copy-done.1) | copy-start | bytes 3145732
  (19 other events, 16.4 us)
